TPU v7x, 128 devices: a whole 4x4x4 slice. The times are simulated.
128 devices in a mesh: img: 16 (over z, y), tile: 8 (over x, core).
Axes of the slice: x: 4, y: 4, z: 4, core: 2. Of those that a mesh axis runs over, the one named last changes fastest.
Arguments:
- spins: float32 [16, 3, 16, 256, 256], P('img', None, None, 'tile'), may hold values from -4.5 to 4.5
- aniso: float32 [16, 256, 256], P(None, 'tile'), may hold values from 0.2 to 2
Outputs:
- path: float32 [16, 3, 16, 256, 256], P('img', None, None, 'tile')
All inputs are finite; a program needn't handle non-finite values.
Results may differ from a plain program's by a relative error of at most 0.0003.
Values sent between devices are 32-bit elements; how exact they have to be, the bound alone decides.
No kernel may reach another device: no remote copies, remote signals or barrier semaphores. Data moves between devices by JAX's collectives and lax.ppermute only.
A program may use at most 128 MiB of HBM per device.

v0:
```python
import jax
import jax.numpy as jnp
from jax import lax
from jax.sharding import Mesh
from jax.sharding import PartitionSpec as P

OUTER = 2
INNER = 3
IMG = ("img_0", "img_1")
TILE = ("tile_0", "tile_1")
IMG_TILE = ("img_0", "img_1", "tile_0", "tile_1")
exchange_coef = 1.0
cubic_coef = 0.5
spring_coef = 20.0
step_scale = 0.25
epsilon = 1e-06


def padded_2(cells, sides, width):
    for axis, dim in sides:
        count = lax.axis_size(axis)
        ends = count - 1
        head = lax.slice_in_dim(cells, 0, width, axis=dim)
        tail = lax.slice_in_dim(cells, cells.shape[dim] - width, cells.shape[dim], axis=dim)
        cells = jnp.concatenate(
            [
                lax.ppermute(tail, axis, [(i, (i + 1) % count) for i in range(ends)]),
                cells,
                lax.ppermute(head, axis, [((i + 1) % count, i) for i in range(ends)]),
            ],
            axis=dim,
        )
    return cells


def from_everyone(shard, axis):
    peers = lax.axis_size(axis)
    return lax.all_to_all(
        jnp.broadcast_to(shard[None], (peers, *shard.shape)), axis, 0, 0, tiled=True
    )


def folded_in_pairs(pieces, combine):
    while len(jax.tree.leaves(pieces)[0]) > 1:
        pieces = jax.vmap(combine)(*(pieces[side::2] for side in (0, 1)))
    return pieces[0]


def carried_in(shard, axis, combine, identity):
    peers, here = (lax.axis_size(axis), lax.axis_index(axis))
    passed = jnp.arange(peers) < here

    def kept(part, zero, own):
        part = jnp.where(
            passed.reshape(-1, *(1 for _ in own.shape)), part, jnp.asarray(zero, own.dtype)
        )
        return part

    pieces = from_everyone(shard, axis)
    return folded_in_pairs(kept(pieces, identity, shard), combine)


def over_copies(shard, axis):
    return from_everyone(shard, axis).sum(axis=0)


def over_axes(shard, axes):
    for axis in axes:
        shard = lax.psum(shard, axis)
    return shard


def laplace(field):
    widths = [(0, 0)] * (field.ndim - 4) + [(0, 0), (1, 1), (0, 0), (1, 1)]
    padded = jnp.pad(field, widths)
    centre = padded[..., 1:-1, 1:-1, 1:-1]
    beside_all = padded[..., 2:, 1:-1, 1:-1] + padded[..., :-2, 1:-1, 1:-1]
    beside_all = beside_all + padded[..., 1:-1, 2:, 1:-1] + padded[..., 1:-1, :-2, 1:-1]
    beside_all = beside_all + padded[..., 1:-1, 1:-1, 2:] + padded[..., 1:-1, 1:-1, :-2]
    return beside_all - 6.0 * centre


def axis_select():
    return (jnp.arange(3) == 2).astype(jnp.float32)[:, None, None, None]


def force_field(middle_ext, coefs):
    middle = middle_ext[..., 1:-1, :]
    square_norm = jnp.sum(middle * middle, axis=-4, keepdims=True)
    return (
        exchange_coef * laplace(middle_ext)
        + coefs * middle * axis_select()
        - cubic_coef * (square_norm - 1.0) * middle
    )


def hessian_point(middle, vector, coefs):
    square_norm = jnp.sum(middle * middle, axis=-4, keepdims=True)
    projected = jnp.sum(middle * vector, axis=-4, keepdims=True)
    return coefs * vector * axis_select() - cubic_coef * (
        (square_norm - 1.0) * vector + 2.0 * middle * projected
    )


def add_pair(earlier, later):
    return earlier + later


def body(spins, aniso):
    local_images = spins.shape[0]
    width_x = spins.shape[3]
    img_count = lax.axis_size(IMG)
    tile_count = lax.axis_size(TILE)
    images = local_images * img_count
    cell_count = float(
        images * spins.shape[1] * spins.shape[2] * width_x * tile_count * spins.shape[4]
    )
    first_image = lax.axis_index(IMG) * local_images
    image_index = first_image + jnp.arange(local_images, dtype=jnp.int32)
    segment_live = (image_index < images - 1).astype(jnp.float32)
    interior = ((image_index > 0) & (image_index < images - 1)).astype(jnp.float32)
    target = image_index.astype(jnp.float32) / (images - 1)
    rim_depth = 1
    cycle_mask = 1.0
    current = spins
    for outer_step in range(OUTER):
        repeated = current
        framed_all = padded_2(repeated, ((IMG, 0), (TILE, 3)), rim_depth)
        before_img = framed_all[:-2]
        own_framed = framed_all[1:-1]
        after_img = framed_all[2:]
        difference = (after_img - own_framed)[..., rim_depth : rim_depth + width_x, :]
        middle_seg = 0.5 * (own_framed + after_img)
        drive_own = force_field(middle_seg, aniso)
        diff_sq = jnp.sum(difference * difference, axis=(1, 2, 3, 4))
        drive_sq = jnp.sum(drive_own * drive_own, axis=(1, 2, 3, 4))
        diff_sq, drive_sq = lax.psum((diff_sq, drive_sq), TILE)
        seg_len = segment_live * jnp.sqrt(diff_sq + epsilon)
        drive_len = segment_live * jnp.sqrt(drive_sq + epsilon)
        offset = carried_in(jnp.sum(seg_len), IMG, add_pair, jnp.float32(0.0))
        path_len, drive_total = (
            over_copies(jnp.sum(seg_len), IMG),
            over_copies(jnp.sum(drive_len), IMG),
        )
        before_arc = offset + jnp.cumsum(seg_len) - seg_len
        time_step = path_len / drive_total
        spring_pull = (
            spring_coef * (before_arc / path_len - target) * (images - 1) / (2.0 * path_len)
        )
        spring_pull = spring_pull[:, None, None, None, None]
        interior_mask = interior[:, None, None, None, None]
        before_core = before_img[..., 1:-1, :]
        after_core = after_img[..., 1:-1, :]
        before_own = before_img[..., rim_depth : rim_depth + width_x, :]
        after_own = after_img[..., rim_depth : rim_depth + width_x, :]
        for inner_step in range(INNER):
            if inner_step == 0:
                own_ext = own_framed
            else:
                own_ext = padded_2(current, ((TILE, 3),), rim_depth)
            own_core = own_ext[..., 1:-1, :]
            middle_a = 0.5 * (before_img + own_ext)
            middle_b = 0.5 * (own_ext + after_img)
            res_a = (
                (own_core - before_core) / time_step - force_field(middle_a, aniso)
            ) * cycle_mask
            res_b = (
                (after_core - own_core) / time_step - force_field(middle_b, aniso)
            ) * cycle_mask
            res_sum = res_a + res_b
            adjoint_lap = laplace(padded_2(res_sum, ((TILE, 3),), 1))
            middle_a_own = middle_a[..., rim_depth : rim_depth + width_x, :]
            middle_b_own = middle_b[..., rim_depth : rim_depth + width_x, :]
            adjoint = exchange_coef * adjoint_lap
            adjoint = (
                adjoint
                + hessian_point(middle_a_own, res_a, aniso)
                + hessian_point(middle_b_own, res_b, aniso)
            )
            gradients = (
                res_a - res_b - 0.5 * time_step * adjoint + spring_pull * (after_own - before_own)
            )
            gradients = gradients * interior_mask
            grad_total = over_axes(jnp.sum(gradients * gradients), IMG_TILE)
            grad_scale = jnp.sqrt(grad_total / cell_count + epsilon)
            current = current - step_scale * gradients / grad_scale
    return current


def solution(mesh):
    split = Mesh(mesh.devices.reshape(4, 4, 4, 2), ("img_0", "img_1", "tile_0", "tile_1"))
    return jax.shard_map(
        body,
        mesh=split,
        in_specs=(P(IMG, None, None, TILE, None), P(None, TILE, None)),
        out_specs=P(IMG, None, None, TILE, None),
        check_vma=False,
    )
```

profile of v0, /device:TPU:1, one launch (start us, length us, event | category | flops | bytes accessed | tf_op | source)
XLA Modules:
  0.0 635.0 jit_solution(12374536469458918659)
XLA Ops:
  7.9 31.6 %collective-permute-done = f32[1,3,16,32,256]{4,2,3,1,0:T(8,128)S(1)} collective-permute-done((f32[1,3,16,32,256]{4,2,3,1,0:T(8,128)S(1)}, f32[1,3,16,32,256]{4,2,3,1,0:T(8,128)S(1)}, u32[]{:S(2)}, u32[]{:S(2)}) %collective-permute-start) | collective-permute-done | bytes 1572896 | tf_op jit(solution)/shard_map/ppermute | solution.py:27
  46.7 4.9 collective-permute-start.2
  69.8 11.1 %all-reduce.19 = (f32[1]{0:T(128)}, f32[1]{0:T(128)}) all-reduce(f32[1]{0:T(128)} %bitcast.1, f32[1]{0:T(128)} %bitcast.3), channel_id=1, replica_groups=mesh['img_0'=4,'img_1'=4,'tile_0'=4,'tile_1'=2] {'tile_0','tile_1'}, use_global_device_ids=true, to_apply=%region_1.2 | all-reduce | flops 2 | bytes 16 | tf_op jit(solution)/shard_map/psum | solution.py:137
  82.7 9.1 %all-to-all-start = ((f32[16,1,1]{2,1,0:T(1,128)}), f32[16,1,1]{2,1,0:T(1,128)S(1)}, u32[]{:S(2)}, u32[]{:S(2)}) async-start(f32[16,1,1]{2,1,0:T(1,128)} %broadcast_in_dim.22), calls=%async_computation | async-start | bytes 16384 | tf_op jit(solution)/shard_map/all_to_all | solution.py:38
  91.9 6.2 all-to-all-done
  103.5 4.9 all-to-all-done.1
  110.4 8.4 %multiply_reduce_fusion.28 = (f32[16,32,256]{2,0,1:T(8,128)S(1)}, f32[1,3,16,32,256]{4,2,3,1,0:T(8,128)S(1)}, f32[16,32,256]{2,0,1:T(8,128)S(1)}, f32[1,3,16,32,256]{4,2,3,1,0:T(8,128)S(1)}) fusion(f32[1,3,16,34,256]{4,2,3,1,0:T(8,128)} %copy-done.2, f32[16,32,256]{2,0,1:T(8,128)S(1)} %get-tuple-element.128, f32[3]{0:T(128)S(1)} %compare_convert_fusion, ...), kind=kLoop, calls=%fused_computation.318 | loop fusion | flops 8388608 | bytes 19496976 | tf_op jit(solution)/shard_map/reduce_sum | solution.py:99
  122.3 6.4 %collective-permute-start.4 = (f32[1,3,16,1,256]{4,2,3,1,0:T(8,128)S(1)}, f32[1,3,16,1,256]{4,2,3,1,0:T(8,128)S(1)}, u32[]{:S(2)}, u32[]{:S(2)}) collective-permute-start(f32[1,3,16,1,256]{4,2,3,1,0:T(8,128)S(1)} %get-tuple-element.103), channel_id=1, source_target_pairs={{0,1},{1,2},{2,3},{3,4},{4,5},{5,6},{6,7},{8,9},{9,10},{10,11},{11... | collective-permute-start | bytes 147464 | tf_op jit(solution)/shard_map/ppermute | solution.py:27
  138.6 7.4 %multiply_reduce_fusion.26 = (f32[]{:T(128)}, f32[1,3,16,32,256]{4,2,3,1,0:T(8,128)}, f32[1,3,16,32,256]{4,2,3,1,0:T(8,128)}) fusion(f32[]{:T(128)} %bitcast.10, f32[16,32,256]{2,0,1:T(8,128)} %broadcast_multiply_fusion.10, f32[1,3,16,34,256]{4,2,3,1,0:T(8,128)S(1)} %get-tuple-element.68, f32[1,3,16,32,256]{4,2,3,1,0:T(8,128)} %copy-done.41, ...), kind=kLoop, calls=%fused_computation.315 | loop fusion | flops 13369343 | bytes 23167004 | tf_op jit(solution)/shard_map/reduce_sum | solution.py:184
  145.9 7.5 %psum.198 = f32[]{:T(128)} all-reduce(f32[]{:T(128)} %get-tuple-element.46), channel_id=1, replica_groups=mesh['img_0'=4,'img_1'=4,'tile_0'=4,'tile_1'=2] {'img_0'}, use_global_device_ids=true, to_apply=%region_11.12 | all-reduce | flops 1 | bytes 8 | tf_op jit(solution)/shard_map/psum | solution.py:69
  153.4 7.7 %psum.199 = f32[]{:T(128)} all-reduce(f32[]{:T(128)} %psum.198), channel_id=1, replica_groups=mesh['img_0'=4,'img_1'=4,'tile_0'=4,'tile_1'=2] {'img_1'}, use_global_device_ids=true, to_apply=%region_12.13 | all-reduce | flops 1 | bytes 8 | tf_op jit(solution)/shard_map/psum | solution.py:69
  161.0 7.3 %psum.200 = f32[]{:T(128)} all-reduce(f32[]{:T(128)} %psum.199), channel_id=1, replica_groups=mesh['img_0'=4,'img_1'=4,'tile_0'=4,'tile_1'=2] {'tile_0'}, use_global_device_ids=true, to_apply=%region_13.14 | all-reduce | flops 1 | bytes 8 | tf_op jit(solution)/shard_map/psum | solution.py:69
  168.3 10.6 %psum.201 = f32[]{:T(128)} all-reduce(f32[]{:T(128)} %psum.200), channel_id=1, replica_groups=mesh['img_0'=4,'img_1'=4,'tile_0'=4,'tile_1'=2] {'tile_1'}, use_global_device_ids=true, to_apply=%region_14.15 | all-reduce | flops 1 | bytes 8 | tf_op jit(solution)/shard_map/psum | solution.py:69
  194.6 7.8 %multiply_reduce_fusion.23 = (f32[16,32,256]{2,0,1:T(8,128)}, f32[1,3,16,32,256]{4,2,3,1,0:T(8,128)}, f32[16,32,256]{2,0,1:T(8,128)}, f32[1,3,16,32,256]{4,2,3,1,0:T(8,128)}) fusion(f32[1,3,16,34,256]{4,2,3,1,0:T(8,128)S(1)} %get-tuple-element.61, f32[16,32,256]{2,0,1:T(8,128)} %get-tuple-element.124, f32[3]{0:T(128)S(1)} %compare_convert_fusion, ...), kind=kLoop, calls=%fused_computation.311 | loop fusion | flops 13107200 | bytes 23265796 | tf_op jit(solution)/shard_map/reduce_sum | solution.py:99
  215.8 4.7 multiply_reduce_fusion.21
  220.6 7.1 %psum.202 = f32[]{:T(128)} all-reduce(f32[]{:T(128)} %get-tuple-element.40), channel_id=1, replica_groups=mesh['img_0'=4,'img_1'=4,'tile_0'=4,'tile_1'=2] {'img_0'}, use_global_device_ids=true, to_apply=%region_20.21 | all-reduce | flops 1 | bytes 8 | tf_op jit(solution)/shard_map/psum | solution.py:69
  227.6 7.3 %psum.203 = f32[]{:T(128)} all-reduce(f32[]{:T(128)} %psum.202), channel_id=1, replica_groups=mesh['img_0'=4,'img_1'=4,'tile_0'=4,'tile_1'=2] {'img_1'}, use_global_device_ids=true, to_apply=%region_21.22 | all-reduce | flops 1 | bytes 8 | tf_op jit(solution)/shard_map/psum | solution.py:69
  235.0 7.1 %psum.204 = f32[]{:T(128)} all-reduce(f32[]{:T(128)} %psum.203), channel_id=1, replica_groups=mesh['img_0'=4,'img_1'=4,'tile_0'=4,'tile_1'=2] {'tile_0'}, use_global_device_ids=true, to_apply=%region_22.23 | all-reduce | flops 1 | bytes 8 | tf_op jit(solution)/shard_map/psum | solution.py:69
  242.1 8.7 %psum.205 = f32[]{:T(128)} all-reduce(f32[]{:T(128)} %psum.204), channel_id=1, replica_groups=mesh['img_0'=4,'img_1'=4,'tile_0'=4,'tile_1'=2] {'tile_1'}, use_global_device_ids=true, to_apply=%region_23.24 | all-reduce | flops 1 | bytes 8 | tf_op jit(solution)/shard_map/psum | solution.py:69
  265.9 7.7 %multiply_reduce_fusion.18 = (f32[16,32,256]{2,0,1:T(8,128)}, f32[1,3,16,32,256]{4,2,3,1,0:T(8,128)}, f32[16,32,256]{2,0,1:T(8,128)}, f32[1,3,16,32,256]{4,2,3,1,0:T(8,128)}) fusion(f32[1,3,16,34,256]{4,2,3,1,0:T(8,128)S(1)} %get-tuple-element.59, f32[16,32,256]{2,0,1:T(8,128)} %get-tuple-element.120, f32[3]{0:T(128)S(1)} %compare_convert_fusion, ...), kind=kLoop, calls=%fused_computation.305 | loop fusion | flops 13107200 | bytes 23265796 | tf_op jit(solution)/shard_map/reduce_sum | solution.py:99
  291.8 7.3 %psum.206 = f32[]{:T(128)} all-reduce(f32[]{:T(128)} %get-tuple-element.34), channel_id=1, replica_groups=mesh['img_0'=4,'img_1'=4,'tile_0'=4,'tile_1'=2] {'img_0'}, use_global_device_ids=true, to_apply=%region_29.30 | all-reduce | flops 1 | bytes 8 | tf_op jit(solution)/shard_map/psum | solution.py:69
  299.1 7.7 %psum.207 = f32[]{:T(128)} all-reduce(f32[]{:T(128)} %psum.206), channel_id=1, replica_groups=mesh['img_0'=4,'img_1'=4,'tile_0'=4,'tile_1'=2] {'img_1'}, use_global_device_ids=true, to_apply=%region_30.31 | all-reduce | flops 1 | bytes 8 | tf_op jit(solution)/shard_map/psum | solution.py:69
  306.8 7.0 %psum.208 = f32[]{:T(128)} all-reduce(f32[]{:T(128)} %psum.207), channel_id=1, replica_groups=mesh['img_0'=4,'img_1'=4,'tile_0'=4,'tile_1'=2] {'tile_0'}, use_global_device_ids=true, to_apply=%region_31.32 | all-reduce | flops 1 | bytes 8 | tf_op jit(solution)/shard_map/psum | solution.py:69
  313.8 8.5 %psum.209 = f32[]{:T(128)} all-reduce(f32[]{:T(128)} %psum.208), channel_id=1, replica_groups=mesh['img_0'=4,'img_1'=4,'tile_0'=4,'tile_1'=2] {'tile_1'}, use_global_device_ids=true, to_apply=%region_32.33 | all-reduce | flops 1 | bytes 8 | tf_op jit(solution)/shard_map/psum | solution.py:69
  330.2 32.1 %collective-permute-done.15 = f32[1,3,16,32,256]{4,2,3,1,0:T(8,128)S(1)} collective-permute-done((f32[1,3,16,32,256]{4,2,3,1,0:T(8,128)S(1)}, f32[1,3,16,32,256]{4,2,3,1,0:T(8,128)S(1)}, u32[]{:S(2)}, u32[]{:S(2)}) %collective-permute-start.15) | collective-permute-done | bytes 1572896 | tf_op jit(solution)/shard_map/ppermute | solution.py:29
  382.0 10.6 %all-reduce.18 = (f32[1]{0:T(128)}, f32[1]{0:T(128)}) all-reduce(f32[1]{0:T(128)} %bitcast.11, f32[1]{0:T(128)} %bitcast.13), channel_id=1, replica_groups=mesh['img_0'=4,'img_1'=4,'tile_0'=4,'tile_1'=2] {'tile_0','tile_1'}, use_global_device_ids=true, to_apply=%region_34.35 | all-reduce | flops 2 | bytes 16 | tf_op jit(solution)/shard_map/psum | solution.py:137
  394.6 6.9 %all-to-all-start.2 = ((f32[16,1,1]{2,1,0:T(1,128)}), f32[16,1,1]{2,1,0:T(1,128)S(1)}, u32[]{:S(2)}, u32[]{:S(2)}) async-start(f32[16,1,1]{2,1,0:T(1,128)} %broadcast_in_dim.27), calls=%async_computation.2 | async-start | bytes 16384 | tf_op jit(solution)/shard_map/all_to_all | solution.py:38
  401.5 6.4 %all-to-all-done.2 = f32[16,1,1]{2,1,0:T(1,128)S(1)} async-done(((f32[16,1,1]{2,1,0:T(1,128)}), f32[16,1,1]{2,1,0:T(1,128)S(1)}, u32[]{:S(2)}, u32[]{:S(2)}) %all-to-all-start.2) | async-done | bytes 96 | tf_op jit(solution)/shard_map/all_to_all | solution.py:38
  413.3 5.1 all-to-all-done.3
  420.3 8.1 %multiply_reduce_fusion.12 = (f32[16,32,256]{2,0,1:T(8,128)S(1)}, f32[1,3,16,32,256]{4,2,3,1,0:T(8,128)S(1)}, f32[16,32,256]{2,0,1:T(8,128)S(1)}, f32[1,3,16,32,256]{4,2,3,1,0:T(8,128)S(1)}) fusion(f32[1,3,16,34,256]{4,2,3,1,0:T(8,128)} %copy-done, f32[16,32,256]{2,0,1:T(8,128)S(1)} %get-tuple-element.116, f32[3]{0:T(128)S(1)} %compare_convert_fusion, ...), kind=kLoop, calls=%fused_computation.297 | loop fusion | flops 8388608 | bytes 19496976 | tf_op jit(solution)/shard_map/reduce_sum | solution.py:99
  432.0 6.5 %collective-permute-start.18 = (f32[1,3,16,1,256]{4,2,3,1,0:T(8,128)S(1)}, f32[1,3,16,1,256]{4,2,3,1,0:T(8,128)S(1)}, u32[]{:S(2)}, u32[]{:S(2)}) collective-permute-start(f32[1,3,16,1,256]{4,2,3,1,0:T(8,128)S(1)} %get-tuple-element.91), channel_id=1, source_target_pairs={{0,1},{1,2},{2,3},{3,4},{4,5},{5,6},{6,7},{8,9},{9,10},{10,11},{11... | collective-permute-start | bytes 147464 | tf_op jit(solution)/shard_map/ppermute | solution.py:27
  448.5 7.3 %multiply_reduce_fusion.10 = (f32[]{:T(128)}, f32[1,3,16,32,256]{4,2,3,1,0:T(8,128)}, f32[1,3,16,32,256]{4,2,3,1,0:T(8,128)}) fusion(f32[]{:T(128)} %bitcast.10, f32[16,32,256]{2,0,1:T(8,128)} %broadcast_multiply_fusion.4, f32[1,3,16,34,256]{4,2,3,1,0:T(8,128)S(1)} %get-tuple-element.64, f32[1,3,16,32,256]{4,2,3,1,0:T(8,128)} %copy-done.39, ...), kind=kLoop, calls=%fused_computation.294 | loop fusion | flops 13369343 | bytes 23167004 | tf_op jit(solution)/shard_map/reduce_sum | solution.py:184
  455.7 7.8 %psum.212 = f32[]{:T(128)} all-reduce(f32[]{:T(128)} %get-tuple-element.25), channel_id=1, replica_groups=mesh['img_0'=4,'img_1'=4,'tile_0'=4,'tile_1'=2] {'img_0'}, use_global_device_ids=true, to_apply=%region_44.45 | all-reduce | flops 1 | bytes 8 | tf_op jit(solution)/shard_map/psum | solution.py:69
  463.5 7.6 %psum.213 = f32[]{:T(128)} all-reduce(f32[]{:T(128)} %psum.212), channel_id=1, replica_groups=mesh['img_0'=4,'img_1'=4,'tile_0'=4,'tile_1'=2] {'img_1'}, use_global_device_ids=true, to_apply=%region_45.46 | all-reduce | flops 1 | bytes 8 | tf_op jit(solution)/shard_map/psum | solution.py:69
  471.2 6.6 %psum.214 = f32[]{:T(128)} all-reduce(f32[]{:T(128)} %psum.213), channel_id=1, replica_groups=mesh['img_0'=4,'img_1'=4,'tile_0'=4,'tile_1'=2] {'tile_0'}, use_global_device_ids=true, to_apply=%region_46.47 | all-reduce | flops 1 | bytes 8 | tf_op jit(solution)/shard_map/psum | solution.py:69
  477.8 9.8 %psum.215 = f32[]{:T(128)} all-reduce(f32[]{:T(128)} %psum.214), channel_id=1, replica_groups=mesh['img_0'=4,'img_1'=4,'tile_0'=4,'tile_1'=2] {'tile_1'}, use_global_device_ids=true, to_apply=%region_47.48 | all-reduce | flops 1 | bytes 8 | tf_op jit(solution)/shard_map/psum | solution.py:69
  502.8 7.7 %multiply_reduce_fusion.7 = (f32[16,32,256]{2,0,1:T(8,128)}, f32[1,3,16,32,256]{4,2,3,1,0:T(8,128)}, f32[16,32,256]{2,0,1:T(8,128)}, f32[1,3,16,32,256]{4,2,3,1,0:T(8,128)}) fusion(f32[1,3,16,34,256]{4,2,3,1,0:T(8,128)S(1)} %get-tuple-element.57, f32[16,32,256]{2,0,1:T(8,128)} %get-tuple-element.112, f32[3]{0:T(128)S(1)} %compare_convert_fusion, ...), kind=kLoop, calls=%fused_computation.290 | loop fusion | flops 13107200 | bytes 23265796 | tf_op jit(solution)/shard_map/reduce_sum | solution.py:99
  523.9 4.7 multiply_reduce_fusion.5
  528.7 7.2 %psum.216 = f32[]{:T(128)} all-reduce(f32[]{:T(128)} %get-tuple-element.19), channel_id=1, replica_groups=mesh['img_0'=4,'img_1'=4,'tile_0'=4,'tile_1'=2] {'img_0'}, use_global_device_ids=true, to_apply=%region_53.54 | all-reduce | flops 1 | bytes 8 | tf_op jit(solution)/shard_map/psum | solution.py:69
  535.9 7.0 %psum.217 = f32[]{:T(128)} all-reduce(f32[]{:T(128)} %psum.216), channel_id=1, replica_groups=mesh['img_0'=4,'img_1'=4,'tile_0'=4,'tile_1'=2] {'img_1'}, use_global_device_ids=true, to_apply=%region_54.55 | all-reduce | flops 1 | bytes 8 | tf_op jit(solution)/shard_map/psum | solution.py:69
  542.9 7.0 %psum.218 = f32[]{:T(128)} all-reduce(f32[]{:T(128)} %psum.217), channel_id=1, replica_groups=mesh['img_0'=4,'img_1'=4,'tile_0'=4,'tile_1'=2] {'tile_0'}, use_global_device_ids=true, to_apply=%region_55.56 | all-reduce | flops 1 | bytes 8 | tf_op jit(solution)/shard_map/psum | solution.py:69
  550.0 8.5 %psum.219 = f32[]{:T(128)} all-reduce(f32[]{:T(128)} %psum.218), channel_id=1, replica_groups=mesh['img_0'=4,'img_1'=4,'tile_0'=4,'tile_1'=2] {'tile_1'}, use_global_device_ids=true, to_apply=%region_56.57 | all-reduce | flops 1 | bytes 8 | tf_op jit(solution)/shard_map/psum | solution.py:69
  573.6 7.7 %multiply_reduce_fusion.2 = (f32[16,32,256]{2,0,1:T(8,128)}, f32[1,3,16,32,256]{4,2,3,1,0:T(8,128)}, f32[16,32,256]{2,0,1:T(8,128)}, f32[1,3,16,32,256]{4,2,3,1,0:T(8,128)}) fusion(f32[1,3,16,34,256]{4,2,3,1,0:T(8,128)S(1)} %get-tuple-element.55, f32[16,32,256]{2,0,1:T(8,128)} %get-tuple-element.108, f32[3]{0:T(128)S(1)} %compare_convert_fusion, ...), kind=kLoop, calls=%fused_computation.284 | loop fusion | flops 13107200 | bytes 23265796 | tf_op jit(solution)/shard_map/reduce_sum | solution.py:99
  594.7 4.7 multiply_reduce_fusion
  599.4 7.7 %psum.220 = f32[]{:T(128)} all-reduce(f32[]{:T(128)} %get-tuple-element.13), channel_id=1, replica_groups=mesh['img_0'=4,'img_1'=4,'tile_0'=4,'tile_1'=2] {'img_0'}, use_global_device_ids=true, to_apply=%region_62.63 | all-reduce | flops 1 | bytes 8 | tf_op jit(solution)/shard_map/psum | solution.py:69
  607.1 7.5 %psum.221 = f32[]{:T(128)} all-reduce(f32[]{:T(128)} %psum.220), channel_id=1, replica_groups=mesh['img_0'=4,'img_1'=4,'tile_0'=4,'tile_1'=2] {'img_1'}, use_global_device_ids=true, to_apply=%region_63.64 | all-reduce | flops 1 | bytes 8 | tf_op jit(solution)/shard_map/psum | solution.py:69
  614.6 7.1 %psum.222 = f32[]{:T(128)} all-reduce(f32[]{:T(128)} %psum.221), channel_id=1, replica_groups=mesh['img_0'=4,'img_1'=4,'tile_0'=4,'tile_1'=2] {'tile_0'}, use_global_device_ids=true, to_apply=%region_64.65 | all-reduce | flops 1 | bytes 8 | tf_op jit(solution)/shard_map/psum | solution.py:69
  621.8 8.5 %psum.223 = f32[]{:T(128)} all-reduce(f32[]{:T(128)} %psum.222), channel_id=1, replica_groups=mesh['img_0'=4,'img_1'=4,'tile_0'=4,'tile_1'=2] {'tile_1'}, use_global_device_ids=true, to_apply=%region_65.66 | all-reduce | flops 1 | bytes 8 | tf_op jit(solution)/shard_map/psum | solution.py:69
  (268 shorter events, 214.3 us)
Async XLA Ops:
  2.3 38.5 %copy-start.23 = (f32[1,3,16,32,256]{4,3,2,1,0:T(8,128)S(1)}, f32[1,3,16,32,256]{4,3,2,1,0:T(8,128)}, u32[]{:S(2)}) copy-start(f32[1,3,16,32,256]{4,3,2,1,0:T(8,128)} %param.2) | copy-start | bytes 4718596
  2.3 37.2 %collective-permute-start = (f32[1,3,16,32,256]{4,2,3,1,0:T(8,128)S(1)}, f32[1,3,16,32,256]{4,2,3,1,0:T(8,128)S(1)}, u32[]{:S(2)}, u32[]{:S(2)}) collective-permute-start(f32[1,3,16,32,256]{4,2,3,1,0:T(8,128)S(1)} %copy.34), channel_id=1, source_target_pairs={{0,8},{8,16},{16,24},{24,32},{32,40},{40,48},{48,56},{56,64},{64,7... | collective-permute-start | bytes 4718600 | tf_op jit(solution)/shard_map/ppermute | solution.py:27
  6.6 36.8 %collective-permute-start.1 = (f32[1,3,16,32,256]{4,2,3,1,0:T(8,128)S(1)}, f32[1,3,16,32,256]{4,2,3,1,0:T(8,128)S(1)}, u32[]{:S(2)}, u32[]{:S(2)}) collective-permute-start(f32[1,3,16,32,256]{4,2,3,1,0:T(8,128)S(1)} %copy.34), channel_id=1, source_target_pairs={{8,0},{16,8},{24,16},{32,24},{40,32},{48,40},{56,48},{64,56},{72,6... | collective-permute-start | bytes 4718600 | tf_op jit(solution)/shard_map/ppermute | solution.py:29
  41.7 11.8 %copy-start.49 = (f32[16,32,256]{2,1,0:T(8,128)S(1)}, f32[16,32,256]{2,1,0:T(8,128)}, u32[]{:S(2)}) copy-start(f32[16,32,256]{2,1,0:T(8,128)} %param.3) | copy-start | bytes 1572868
  46.7 7.2 %collective-permute-start.2 = (f32[3,3,16,1,256]{4,2,3,1,0:T(8,128)S(1)}, f32[3,3,16,1,256]{4,2,3,1,0:T(8,128)S(1)}, u32[]{:S(2)}, u32[]{:S(2)}) collective-permute-start(f32[3,3,16,1,256]{4,2,3,1,0:T(8,128)S(1)} %get-tuple-element.73), channel_id=1, source_target_pairs={{0,1},{1,2},{2,3},{3,4},{4,5},{5,6},{6,7},{8,9},{9,10},{10,11},{11... | collective-permute-start | bytes 442376 | tf_op jit(solution)/shard_map/ppermute | solution.py:27
  51.6 6.5 %collective-permute-start.3 = (f32[3,3,16,1,256]{4,2,3,1,0:T(8,128)S(1)}, f32[3,3,16,1,256]{4,2,3,1,0:T(8,128)S(1)}, u32[]{:S(2)}, u32[]{:S(2)}) collective-permute-start(f32[3,3,16,1,256]{4,2,3,1,0:T(8,128)S(1)} %get-tuple-element.74), channel_id=1, source_target_pairs={{1,0},{2,1},{3,2},{4,3},{5,4},{6,5},{7,6},{9,8},{10,9},{11,10},{12... | collective-permute-start | bytes 442376 | tf_op jit(solution)/shard_map/ppermute | solution.py:29
  82.7 15.4 %all-to-all-start = ((f32[16,1,1]{2,1,0:T(1,128)}), f32[16,1,1]{2,1,0:T(1,128)S(1)}, u32[]{:S(2)}, u32[]{:S(2)}) async-start(f32[16,1,1]{2,1,0:T(1,128)} %broadcast_in_dim.22), calls=%async_computation | async-start | bytes 16384 | tf_op jit(solution)/shard_map/all_to_all | solution.py:38
  98.8 9.6 %all-to-all-start.1 = ((f32[16,1,1]{2,1,0:T(1,128)}), f32[16,1,1]{2,1,0:T(1,128)S(1)}, u32[]{:S(2)}, u32[]{:S(2)}) async-start(f32[16,1,1]{2,1,0:T(1,128)} %broadcast_in_dim.24), calls=%async_computation.1 | async-start | bytes 16384 | tf_op jit(solution)/shard_map/all_to_all | solution.py:38
  122.3 12.1 %collective-permute-start.4 = (f32[1,3,16,1,256]{4,2,3,1,0:T(8,128)S(1)}, f32[1,3,16,1,256]{4,2,3,1,0:T(8,128)S(1)}, u32[]{:S(2)}, u32[]{:S(2)}) collective-permute-start(f32[1,3,16,1,256]{4,2,3,1,0:T(8,128)S(1)} %get-tuple-element.103), channel_id=1, source_target_pairs={{0,1},{1,2},{2,3},{3,4},{4,5},{5,6},{6,7},{8,9},{9,10},{10,11},{11... | collective-permute-start | bytes 147464 | tf_op jit(solution)/shard_map/ppermute | solution.py:27
  128.7 5.7 collective-permute-start.5
  182.5 9.9 %copy-start.22 = (f32[1,3,16,32,256]{4,2,3,1,0:T(8,128)}, f32[1,3,16,32,256]{4,2,3,1,0:T(8,128)S(1)}, u32[]{:S(2)}) copy-start(f32[1,3,16,32,256]{4,2,3,1,0:T(8,128)S(1)} %divide_subtract_fusion.6) | copy-start | bytes 4718596
  182.5 4.3 collective-permute-start.6
  184.5 5.4 collective-permute-start.7
  203.5 6.7 %copy-start.45 = (f32[16,32,256]{2,0,1:T(8,128)S(1)}, f32[16,32,256]{2,0,1:T(8,128)}, u32[]{:S(2)}) copy-start(f32[16,32,256]{2,0,1:T(8,128)} %get-tuple-element.81) | copy-start | bytes 1572868
  205.8 4.4 collective-permute-start.8
  207.7 5.4 collective-permute-start.9
  210.2 5.6 copy-start.30
  253.7 10.0 %copy-start.19 = (f32[1,3,16,32,256]{4,2,3,1,0:T(8,128)}, f32[1,3,16,32,256]{4,2,3,1,0:T(8,128)S(1)}, u32[]{:S(2)}) copy-start(f32[1,3,16,32,256]{4,2,3,1,0:T(8,128)S(1)} %divide_subtract_fusion.5) | copy-start | bytes 4718596
  253.7 4.3 collective-permute-start.10
  255.7 5.4 collective-permute-start.11
  274.7 6.7 %copy-start.43 = (f32[16,32,256]{2,0,1:T(8,128)S(1)}, f32[16,32,256]{2,0,1:T(8,128)}, u32[]{:S(2)}) copy-start(f32[16,32,256]{2,0,1:T(8,128)} %get-tuple-element.79) | copy-start | bytes 1572868
  277.0 4.4 collective-permute-start.12
  278.9 5.4 collective-permute-start.13
  287.1 35.9 %copy-start.20 = (f32[1,3,16,32,256]{4,2,3,1,0:T(8,128)S(1)}, f32[1,3,16,32,256]{4,2,3,1,0:T(8,128)}, u32[]{:S(2)}) copy-start(f32[1,3,16,32,256]{4,2,3,1,0:T(8,128)} %copy-done.19) | copy-start | bytes 4718596
  324.8 48.0 %copy-start.11 = (f32[1,3,16,32,256]{4,2,3,1,0:T(8,128)}, f32[1,3,16,32,256]{4,2,3,1,0:T(8,128)S(1)}, u32[]{:S(2)}) copy-start(f32[1,3,16,32,256]{4,2,3,1,0:T(8,128)S(1)} %divide_subtract_fusion.4) | copy-start | bytes 4718596
  324.8 37.5 %collective-permute-start.15 = (f32[1,3,16,32,256]{4,2,3,1,0:T(8,128)S(1)}, f32[1,3,16,32,256]{4,2,3,1,0:T(8,128)S(1)}, u32[]{:S(2)}, u32[]{:S(2)}) collective-permute-start(f32[1,3,16,32,256]{4,2,3,1,0:T(8,128)S(1)} %divide_subtract_fusion.4), channel_id=1, source_target_pairs={{8,0},{16,8},{24,16},{32,24},{40,32},{48,40},{56,48},{64,56},{72,6... | collective-permute-start | bytes 4718600 | tf_op jit(solution)/shard_map/ppermute | solution.py:29
  326.1 37.1 %collective-permute-start.14 = (f32[1,3,16,32,256]{4,2,3,1,0:T(8,128)S(1)}, f32[1,3,16,32,256]{4,2,3,1,0:T(8,128)S(1)}, u32[]{:S(2)}, u32[]{:S(2)}) collective-permute-start(f32[1,3,16,32,256]{4,2,3,1,0:T(8,128)S(1)} %divide_subtract_fusion.4), channel_id=1, source_target_pairs={{0,8},{8,16},{16,24},{24,32},{32,40},{40,48},{48,56},{56,64},{64,7... | collective-permute-start | bytes 4718600 | tf_op jit(solution)/shard_map/ppermute | solution.py:27
  362.3 10.4 %copy-start.4 = (f32[1,3,16,32,256]{4,2,3,1,0:T(8,128)}, f32[1,3,16,32,256]{4,2,3,1,0:T(8,128)S(1)}, u32[]{:S(2)}) copy-start(f32[1,3,16,32,256]{4,2,3,1,0:T(8,128)S(1)} %collective-permute-done.15) | copy-start | bytes 4718596
  363.2 9.6 %copy-start.7 = (f32[1,3,16,32,256]{4,2,3,1,0:T(8,128)}, f32[1,3,16,32,256]{4,2,3,1,0:T(8,128)S(1)}, u32[]{:S(2)}) copy-start(f32[1,3,16,32,256]{4,2,3,1,0:T(8,128)S(1)} %collective-permute-done.14) | copy-start | bytes 4718596
  363.2 5.2 collective-permute-start.16
  366.3 6.5 %collective-permute-start.17 = (f32[3,3,16,1,256]{4,2,3,1,0:T(8,128)S(1)}, f32[3,3,16,1,256]{4,2,3,1,0:T(8,128)S(1)}, u32[]{:S(2)}, u32[]{:S(2)}) collective-permute-start(f32[3,3,16,1,256]{4,2,3,1,0:T(8,128)S(1)} %get-tuple-element.72), channel_id=1, source_target_pairs={{1,0},{2,1},{3,2},{4,3},{5,4},{6,5},{7,6},{9,8},{10,9},{11,10},{12... | collective-permute-start | bytes 442376 | tf_op jit(solution)/shard_map/ppermute | solution.py:29
  394.6 13.3 %all-to-all-start.2 = ((f32[16,1,1]{2,1,0:T(1,128)}), f32[16,1,1]{2,1,0:T(1,128)S(1)}, u32[]{:S(2)}, u32[]{:S(2)}) async-start(f32[16,1,1]{2,1,0:T(1,128)} %broadcast_in_dim.27), calls=%async_computation.2 | async-start | bytes 16384 | tf_op jit(solution)/shard_map/all_to_all | solution.py:38
  408.5 9.8 %all-to-all-start.3 = ((f32[16,1,1]{2,1,0:T(1,128)}), f32[16,1,1]{2,1,0:T(1,128)S(1)}, u32[]{:S(2)}, u32[]{:S(2)}) async-start(f32[16,1,1]{2,1,0:T(1,128)} %broadcast_in_dim.29), calls=%async_computation.3 | async-start | bytes 16384 | tf_op jit(solution)/shard_map/all_to_all | solution.py:38
  432.0 12.3 %collective-permute-start.18 = (f32[1,3,16,1,256]{4,2,3,1,0:T(8,128)S(1)}, f32[1,3,16,1,256]{4,2,3,1,0:T(8,128)S(1)}, u32[]{:S(2)}, u32[]{:S(2)}) collective-permute-start(f32[1,3,16,1,256]{4,2,3,1,0:T(8,128)S(1)} %get-tuple-element.91), channel_id=1, source_target_pairs={{0,1},{1,2},{2,3},{3,4},{4,5},{5,6},{6,7},{8,9},{9,10},{10,11},{11... | collective-permute-start | bytes 147464 | tf_op jit(solution)/shard_map/ppermute | solution.py:27
  438.5 5.9 collective-permute-start.19
  490.6 10.0 %copy-start.21 = (f32[1,3,16,32,256]{4,2,3,1,0:T(8,128)}, f32[1,3,16,32,256]{4,2,3,1,0:T(8,128)S(1)}, u32[]{:S(2)}) copy-start(f32[1,3,16,32,256]{4,2,3,1,0:T(8,128)S(1)} %divide_subtract_fusion.2) | copy-start | bytes 4718596
  490.6 4.3 collective-permute-start.20
  492.6 5.4 collective-permute-start.21
  511.6 6.8 %copy-start.46 = (f32[16,32,256]{2,0,1:T(8,128)S(1)}, f32[16,32,256]{2,0,1:T(8,128)}, u32[]{:S(2)}) copy-start(f32[16,32,256]{2,0,1:T(8,128)} %get-tuple-element.77) | copy-start | bytes 1572868
  513.9 4.6 collective-permute-start.22
  515.8 5.4 collective-permute-start.23
  561.4 10.0 %copy-start.17 = (f32[1,3,16,32,256]{4,2,3,1,0:T(8,128)}, f32[1,3,16,32,256]{4,2,3,1,0:T(8,128)S(1)}, u32[]{:S(2)}) copy-start(f32[1,3,16,32,256]{4,2,3,1,0:T(8,128)S(1)} %divide_subtract_fusion.1) | copy-start | bytes 4718596
  561.5 4.3 collective-permute-start.24
  563.4 5.4 collective-permute-start.25
  582.3 6.7 %copy-start.44 = (f32[16,32,256]{2,0,1:T(8,128)S(1)}, f32[16,32,256]{2,0,1:T(8,128)}, u32[]{:S(2)}) copy-start(f32[16,32,256]{2,0,1:T(8,128)} %get-tuple-element.75) | copy-start | bytes 1572868
  584.6 4.4 collective-permute-start.26
  586.6 5.4 collective-permute-start.27
  594.7 36.3 %copy-start.18 = (f32[1,3,16,32,256]{4,2,3,1,0:T(8,128)S(1)}, f32[1,3,16,32,256]{4,2,3,1,0:T(8,128)}, u32[]{:S(2)}) copy-start(f32[1,3,16,32,256]{4,2,3,1,0:T(8,128)} %copy-done.17) | copy-start | bytes 4718596
  (34 other events, 121.5 us)
where the time goes:
time: 644 us; the launch traced here: 635 us
  blocking collectives  208 us (32%)
  other arithmetic  169 us (26%)
  waiting for transfers between devices  121 us (19%)
  starting transfers between devices  98.1 us (15%)
  local copies, waits for them, and re-layouts  22.4 us (3%)
  between operations  16.4 us (3%)
    psum x24, blocking collectives, over_axes(): shard = lax.psum(shard, axis)  186 us
    ppermute x14, waiting for transfers between devices, padded_2(): lax.ppermute(head, axis, [((i + 1) % count, i) for i in range(ends)])  65.9 us
    reduce_sum x6, other arithmetic, hessian_point(): projected = jnp.sum(middle * vector, axis=-4, keepdims=True)  47.5 us
    ppermute x14, starting transfers between devices, padded_2(): lax.ppermute(tail, axis, [(i, (i + 1) % count) for i in range(ends)])  44.6 us
    reduce_sum x6, other arithmetic, body(): grad_total = over_axes(jnp.sum(gradients * gradients), IMG_TILE)  33.5 us
    ppermute x14, waiting for transfers between devices, padded_2(): lax.ppermute(tail, axis, [(i, (i + 1) % count) for i in range(ends)])  32.7 us
    ppermute x14, starting transfers between devices, padded_2(): lax.ppermute(head, axis, [((i + 1) % count, i) for i in range(ends)])  30.5 us
    all_to_all x4, starting transfers between devices, from_everyone(): lax.all_to_all(jnp.broadcast_to(shard[None], (peers, *shard.shape)), axis...  23 us
  transfers between devices with their start and end apart: 32, of which 19 were waited for; matrix products, arithmetic and copies ran while one was open for 1% of the time, Pallas kernels for 0%

commit v1 on v0

--- a/solution.py
+++ b/solution.py
@@ -66,7 +66,7 @@
 
 def over_axes(shard, axes):
     for axis in axes:
-        shard = lax.psum(shard, axis)
+        shard = jnp.sum(lax.all_gather(shard, axis), axis=0)
     return shard
 
 

time: 644 us -> 671 us (1.042)
  local copies, waits for them, and re-layouts: 22.4 us -> 54.4 us
  other arithmetic: 169 us -> 185 us
  blocking collectives: 208 us -> 192 us
    psum x24 -> x0, blocking collectives: 186 us -> none  [over_axes(): shard = lax.psum(shard, axis)]
    unnamed x0 -> x24, blocking collectives: none -> 170 us
    unnamed x104 -> x168, local copies, waits for them, and re-layouts: 15.3 us -> 47.3 us
    ppermute x14, waiting for transfers between devices: 32.7 us -> 63.8 us  [padded_2(): lax.ppermute(tail, axis, [(i, (i + 1) % count) for i in range(ends)])]
    ppermute x14, waiting for transfers between devices: 65.9 us -> 36.3 us  [padded_2(): lax.ppermute(head, axis, [((i + 1) % count, i) for i in range(ends)])]
    reduce_sum x0 -> x24, other arithmetic: none -> 14.7 us  [over_axes(): shard = jnp.sum(lax.all_gather(shard, axis), axis=0)]
  transfers between devices with their start and end apart: 32 -> 32, of which waited for: 19 -> 19; matrix products, arithmetic and copies ran while one was open for 1% -> 2% of each run, Pallas kernels for 0% -> 0%
where the time goes in v1:
time: 671 us; the launch traced here: 661 us
  blocking collectives  192 us (29%)
  other arithmetic  185 us (28%)
  waiting for transfers between devices  116 us (17%)
  starting transfers between devices  97.2 us (14%)
  local copies, waits for them, and re-layouts  54.4 us (8%)
  between operations  16.5 us (2%)
    unnamed x24, blocking collectives  170 us
    ppermute x14, waiting for transfers between devices, padded_2(): lax.ppermute(tail, axis, [(i, (i + 1) % count) for i in range(ends)])  63.8 us
    reduce_sum x6, other arithmetic, hessian_point(): projected = jnp.sum(middle * vector, axis=-4, keepdims=True)  47.7 us
    unnamed x168, local copies, waits for them, and re-layouts  47.3 us
    ppermute x14, starting transfers between devices, padded_2(): lax.ppermute(tail, axis, [(i, (i + 1) % count) for i in range(ends)])  42.9 us
    ppermute x14, waiting for transfers between devices, padded_2(): lax.ppermute(head, axis, [((i + 1) % count, i) for i in range(ends)])  36.3 us
    reduce_sum x6, other arithmetic, body(): grad_total = over_axes(jnp.sum(gradients * gradients), IMG_TILE)  33.4 us
    ppermute x14, starting transfers between devices, padded_2(): lax.ppermute(head, axis, [((i + 1) % count, i) for i in range(ends)])  31 us
  transfers between devices with their start and end apart: 32, of which 19 were waited for; matrix products, arithmetic and copies ran while one was open for 2% of the time, Pallas kernels for 0%

profile of v1, /device:TPU:1, one launch (start us, length us, event | category | flops | bytes accessed | tf_op | source)
XLA Modules:
  0.0 661.3 jit_solution(2426854586880087857)
XLA Ops:
  7.9 31.6 %collective-permute-done = f32[1,3,16,32,256]{4,2,3,1,0:T(8,128)S(1)} collective-permute-done((f32[1,3,16,32,256]{4,2,3,1,0:T(8,128)S(1)}, f32[1,3,16,32,256]{4,2,3,1,0:T(8,128)S(1)}, u32[]{:S(2)}, u32[]{:S(2)}) %collective-permute-start) | collective-permute-done | bytes 1572896 | tf_op jit(solution)/shard_map/ppermute | solution.py:27
  44.6 4.9 collective-permute-start.2
  65.9 11.1 %all-reduce.43 = (f32[1]{0:T(128)}, f32[1]{0:T(128)}) all-reduce(f32[1]{0:T(128)} %bitcast.1, f32[1]{0:T(128)} %bitcast.3), channel_id=1, replica_groups=mesh['img_0'=4,'img_1'=4,'tile_0'=4,'tile_1'=2] {'tile_0','tile_1'}, use_global_device_ids=true, to_apply=%region_1.2 | all-reduce | flops 2 | bytes 16 | tf_op jit(solution)/shard_map/psum | solution.py:137
  78.3 9.1 %all-to-all-start = ((f32[16,1,1]{2,1,0:T(1,128)}), f32[16,1,1]{2,1,0:T(1,128)S(1)}, u32[]{:S(2)}, u32[]{:S(2)}) async-start(f32[16,1,1]{2,1,0:T(1,128)} %broadcast_in_dim.22), calls=%async_computation | async-start | bytes 16384 | tf_op jit(solution)/shard_map/all_to_all | solution.py:38
  99.4 5.0 all-to-all-done.1
  106.3 8.5 %multiply_reduce_fusion.28 = (f32[16,32,256]{2,0,1:T(8,128)S(1)}, f32[1,3,16,32,256]{4,2,3,1,0:T(8,128)S(1)}, f32[16,32,256]{2,0,1:T(8,128)S(1)}, f32[1,3,16,32,256]{4,2,3,1,0:T(8,128)S(1)}) fusion(f32[1,3,16,34,256]{4,2,3,1,0:T(8,128)} %get-tuple-element.67, f32[16,32,256]{2,0,1:T(8,128)S(1)} %get-tuple-element.128, f32[3]{0:T(128)S(1)} %compare_convert_fusion, ...), kind=kLoop, calls=%fused_computation.318 | loop fusion | flops 8388608 | bytes 19496976 | tf_op jit(solution)/shard_map/reduce_sum | solution.py:99
  117.6 5.9 collective-permute-start.4
  135.2 7.2 %multiply_reduce_fusion.26 = (f32[]{:T(128)}, f32[1,3,16,32,256]{4,2,3,1,0:T(8,128)}, f32[1,3,16,32,256]{4,2,3,1,0:T(8,128)}) fusion(f32[]{:T(128)} %bitcast.10, f32[16,32,256]{2,0,1:T(8,128)} %broadcast_multiply_fusion.10, f32[1,3,16,34,256]{4,2,3,1,0:T(8,128)S(1)} %get-tuple-element.68, f32[1,3,16,32,256]{4,2,3,1,0:T(8,128)} %copy-done.39, ...), kind=kLoop, calls=%fused_computation.315 | loop fusion | flops 13369343 | bytes 23167004 | tf_op jit(solution)/shard_map/reduce_sum | solution.py:184
  144.4 6.8 %all-reduce.18 = f32[4]{0:T(128)S(1)} all-reduce(f32[4]{0:T(128)S(1)} %dynamic-update-slice), channel_id=1, replica_groups=mesh['img_0'=4,'img_1'=4,'tile_0'=4,'tile_1'=2] {'img_0'}, use_global_device_ids=true, to_apply=%add.18 | all-reduce | flops 4 | bytes 32
  153.7 7.0 %all-reduce.19 = f32[4]{0:T(128)S(1)} all-reduce(f32[4]{0:T(128)S(1)} %dynamic-update-slice.1), channel_id=1, replica_groups=mesh['img_0'=4,'img_1'=4,'tile_0'=4,'tile_1'=2] {'img_1'}, use_global_device_ids=true, to_apply=%add.19 | all-reduce | flops 4 | bytes 32
  163.4 6.6 %all-reduce.20 = f32[4]{0:T(128)S(1)} all-reduce(f32[4]{0:T(128)S(1)} %dynamic-update-slice.2), channel_id=1, replica_groups=mesh['img_0'=4,'img_1'=4,'tile_0'=4,'tile_1'=2] {'tile_0'}, use_global_device_ids=true, to_apply=%add.20 | all-reduce | flops 4 | bytes 32
  172.0 9.9 %all-reduce.21 = f32[2]{0:T(128)S(1)} all-reduce(f32[2]{0:T(128)S(1)} %dynamic-update-slice.3), channel_id=1, replica_groups=mesh['img_0'=4,'img_1'=4,'tile_0'=4,'tile_1'=2] {'tile_1'}, use_global_device_ids=true, to_apply=%add.21 | all-reduce | flops 2 | bytes 16
  198.7 7.8 %multiply_reduce_fusion.23 = (f32[16,32,256]{2,0,1:T(8,128)}, f32[1,3,16,32,256]{4,2,3,1,0:T(8,128)}, f32[16,32,256]{2,0,1:T(8,128)}, f32[1,3,16,32,256]{4,2,3,1,0:T(8,128)}) fusion(f32[1,3,16,34,256]{4,2,3,1,0:T(8,128)S(1)} %get-tuple-element.61, f32[16,32,256]{2,0,1:T(8,128)} %get-tuple-element.124, f32[3]{0:T(128)S(1)} %compare_convert_fusion, ...), kind=kLoop, calls=%fused_computation.311 | loop fusion | flops 13107200 | bytes 23265796 | tf_op jit(solution)/shard_map/reduce_sum | solution.py:99
  218.9 4.7 multiply_reduce_fusion.21
  225.0 6.4 all-reduce.22
  233.3 6.7 %all-reduce.23 = f32[4]{0:T(128)S(1)} all-reduce(f32[4]{0:T(128)S(1)} %dynamic-update-slice.5), channel_id=1, replica_groups=mesh['img_0'=4,'img_1'=4,'tile_0'=4,'tile_1'=2] {'img_1'}, use_global_device_ids=true, to_apply=%add.23 | all-reduce | flops 4 | bytes 32
  241.9 6.4 all-reduce.24
  250.4 7.8 %all-reduce.25 = f32[2]{0:T(128)S(1)} all-reduce(f32[2]{0:T(128)S(1)} %dynamic-update-slice.7), channel_id=1, replica_groups=mesh['img_0'=4,'img_1'=4,'tile_0'=4,'tile_1'=2] {'tile_1'}, use_global_device_ids=true, to_apply=%add.25 | all-reduce | flops 2 | bytes 16
  273.9 7.7 %multiply_reduce_fusion.18 = (f32[16,32,256]{2,0,1:T(8,128)}, f32[1,3,16,32,256]{4,2,3,1,0:T(8,128)}, f32[16,32,256]{2,0,1:T(8,128)}, f32[1,3,16,32,256]{4,2,3,1,0:T(8,128)}) fusion(f32[1,3,16,34,256]{4,2,3,1,0:T(8,128)S(1)} %get-tuple-element.59, f32[16,32,256]{2,0,1:T(8,128)} %get-tuple-element.120, f32[3]{0:T(128)S(1)} %compare_convert_fusion, ...), kind=kLoop, calls=%fused_computation.305 | loop fusion | flops 13107200 | bytes 23265796 | tf_op jit(solution)/shard_map/reduce_sum | solution.py:99
  294.1 4.7 multiply_reduce_fusion.16
  300.1 6.7 %all-reduce.26 = f32[4]{0:T(128)S(1)} all-reduce(f32[4]{0:T(128)S(1)} %dynamic-update-slice.8), channel_id=1, replica_groups=mesh['img_0'=4,'img_1'=4,'tile_0'=4,'tile_1'=2] {'img_0'}, use_global_device_ids=true, to_apply=%add.26 | all-reduce | flops 4 | bytes 32
  308.6 7.0 %all-reduce.27 = f32[4]{0:T(128)S(1)} all-reduce(f32[4]{0:T(128)S(1)} %dynamic-update-slice.9), channel_id=1, replica_groups=mesh['img_0'=4,'img_1'=4,'tile_0'=4,'tile_1'=2] {'img_1'}, use_global_device_ids=true, to_apply=%add.27 | all-reduce | flops 4 | bytes 32
  317.8 6.4 all-reduce.28
  326.1 7.9 %all-reduce.29 = f32[2]{0:T(128)S(1)} all-reduce(f32[2]{0:T(128)S(1)} %dynamic-update-slice.11), channel_id=1, replica_groups=mesh['img_0'=4,'img_1'=4,'tile_0'=4,'tile_1'=2] {'tile_1'}, use_global_device_ids=true, to_apply=%add.29 | all-reduce | flops 2 | bytes 16
  340.7 32.0 %collective-permute-done.14 = f32[1,3,16,32,256]{4,2,3,1,0:T(8,128)S(1)} collective-permute-done((f32[1,3,16,32,256]{4,2,3,1,0:T(8,128)S(1)}, f32[1,3,16,32,256]{4,2,3,1,0:T(8,128)S(1)}, u32[]{:S(2)}, u32[]{:S(2)}) %collective-permute-start.14) | collective-permute-done | bytes 1572896 | tf_op jit(solution)/shard_map/ppermute | solution.py:27
  381.8 4.4 collective-permute-done.17
  394.1 10.1 %all-reduce.42 = (f32[1]{0:T(128)}, f32[1]{0:T(128)}) all-reduce(f32[1]{0:T(128)} %bitcast.27, f32[1]{0:T(128)} %bitcast.29), channel_id=1, replica_groups=mesh['img_0'=4,'img_1'=4,'tile_0'=4,'tile_1'=2] {'tile_0','tile_1'}, use_global_device_ids=true, to_apply=%region_34.35 | all-reduce | flops 2 | bytes 16 | tf_op jit(solution)/shard_map/psum | solution.py:137
  405.5 6.7 %all-to-all-start.2 = ((f32[16,1,1]{2,1,0:T(1,128)}), f32[16,1,1]{2,1,0:T(1,128)S(1)}, u32[]{:S(2)}, u32[]{:S(2)}) async-start(f32[16,1,1]{2,1,0:T(1,128)} %broadcast_in_dim.27), calls=%async_computation.2 | async-start | bytes 16384 | tf_op jit(solution)/shard_map/all_to_all | solution.py:38
  424.1 5.1 all-to-all-done.3
  431.2 8.2 %multiply_reduce_fusion.12 = (f32[16,32,256]{2,0,1:T(8,128)S(1)}, f32[1,3,16,32,256]{4,2,3,1,0:T(8,128)S(1)}, f32[16,32,256]{2,0,1:T(8,128)S(1)}, f32[1,3,16,32,256]{4,2,3,1,0:T(8,128)S(1)}) fusion(f32[1,3,16,34,256]{4,2,3,1,0:T(8,128)} %get-tuple-element.63, f32[16,32,256]{2,0,1:T(8,128)S(1)} %get-tuple-element.116, f32[3]{0:T(128)S(1)} %compare_convert_fusion, ...), kind=kLoop, calls=%fused_computation.297 | loop fusion | flops 8388608 | bytes 19496976 | tf_op jit(solution)/shard_map/reduce_sum | solution.py:99
  442.2 6.3 collective-permute-start.18
  460.2 7.3 %multiply_reduce_fusion.10 = (f32[]{:T(128)}, f32[1,3,16,32,256]{4,2,3,1,0:T(8,128)}, f32[1,3,16,32,256]{4,2,3,1,0:T(8,128)}) fusion(f32[]{:T(128)} %bitcast.10, f32[16,32,256]{2,0,1:T(8,128)} %broadcast_multiply_fusion.4, f32[1,3,16,34,256]{4,2,3,1,0:T(8,128)S(1)} %get-tuple-element.64, f32[1,3,16,32,256]{4,2,3,1,0:T(8,128)} %copy-done.37, ...), kind=kLoop, calls=%fused_computation.294 | loop fusion | flops 13369343 | bytes 23167004 | tf_op jit(solution)/shard_map/reduce_sum | solution.py:184
  468.8 7.1 %all-reduce.30 = f32[4]{0:T(128)S(1)} all-reduce(f32[4]{0:T(128)S(1)} %dynamic-update-slice.12), channel_id=1, replica_groups=mesh['img_0'=4,'img_1'=4,'tile_0'=4,'tile_1'=2] {'img_0'}, use_global_device_ids=true, to_apply=%add.30 | all-reduce | flops 4 | bytes 32
  477.8 7.0 %all-reduce.31 = f32[4]{0:T(128)S(1)} all-reduce(f32[4]{0:T(128)S(1)} %dynamic-update-slice.13), channel_id=1, replica_groups=mesh['img_0'=4,'img_1'=4,'tile_0'=4,'tile_1'=2] {'img_1'}, use_global_device_ids=true, to_apply=%add.31 | all-reduce | flops 4 | bytes 32
  486.8 6.0 all-reduce.32
  494.7 9.4 %all-reduce.33 = f32[2]{0:T(128)S(1)} all-reduce(f32[2]{0:T(128)S(1)} %dynamic-update-slice.15), channel_id=1, replica_groups=mesh['img_0'=4,'img_1'=4,'tile_0'=4,'tile_1'=2] {'tile_1'}, use_global_device_ids=true, to_apply=%add.33 | all-reduce | flops 2 | bytes 16
  520.3 7.8 %multiply_reduce_fusion.7 = (f32[16,32,256]{2,0,1:T(8,128)}, f32[1,3,16,32,256]{4,2,3,1,0:T(8,128)}, f32[16,32,256]{2,0,1:T(8,128)}, f32[1,3,16,32,256]{4,2,3,1,0:T(8,128)}) fusion(f32[1,3,16,34,256]{4,2,3,1,0:T(8,128)S(1)} %get-tuple-element.57, f32[16,32,256]{2,0,1:T(8,128)} %get-tuple-element.112, f32[3]{0:T(128)S(1)} %compare_convert_fusion, ...), kind=kLoop, calls=%fused_computation.290 | loop fusion | flops 13107200 | bytes 23265796 | tf_op jit(solution)/shard_map/reduce_sum | solution.py:99
  540.6 4.7 multiply_reduce_fusion.5
  546.6 6.6 all-reduce.34
  555.1 6.4 all-reduce.35
  563.5 6.4 all-reduce.36
  571.8 7.8 %all-reduce.37 = f32[2]{0:T(128)S(1)} all-reduce(f32[2]{0:T(128)S(1)} %dynamic-update-slice.19), channel_id=1, replica_groups=mesh['img_0'=4,'img_1'=4,'tile_0'=4,'tile_1'=2] {'tile_1'}, use_global_device_ids=true, to_apply=%add.37 | all-reduce | flops 2 | bytes 16
  595.3 7.7 %multiply_reduce_fusion.2 = (f32[16,32,256]{2,0,1:T(8,128)}, f32[1,3,16,32,256]{4,2,3,1,0:T(8,128)}, f32[16,32,256]{2,0,1:T(8,128)}, f32[1,3,16,32,256]{4,2,3,1,0:T(8,128)}) fusion(f32[1,3,16,34,256]{4,2,3,1,0:T(8,128)S(1)} %get-tuple-element.55, f32[16,32,256]{2,0,1:T(8,128)} %get-tuple-element.108, f32[3]{0:T(128)S(1)} %compare_convert_fusion, ...), kind=kLoop, calls=%fused_computation.284 | loop fusion | flops 13107200 | bytes 23265796 | tf_op jit(solution)/shard_map/reduce_sum | solution.py:99
  615.5 4.7 multiply_reduce_fusion
  621.6 7.0 %all-reduce.38 = f32[4]{0:T(128)S(1)} all-reduce(f32[4]{0:T(128)S(1)} %dynamic-update-slice.20), channel_id=1, replica_groups=mesh['img_0'=4,'img_1'=4,'tile_0'=4,'tile_1'=2] {'img_0'}, use_global_device_ids=true, to_apply=%add.38 | all-reduce | flops 4 | bytes 32
  630.5 6.8 %all-reduce.39 = f32[4]{0:T(128)S(1)} all-reduce(f32[4]{0:T(128)S(1)} %dynamic-update-slice.21), channel_id=1, replica_groups=mesh['img_0'=4,'img_1'=4,'tile_0'=4,'tile_1'=2] {'img_1'}, use_global_device_ids=true, to_apply=%add.39 | all-reduce | flops 4 | bytes 32
  639.4 6.4 all-reduce.40
  647.9 7.8 %all-reduce.41 = f32[2]{0:T(128)S(1)} all-reduce(f32[2]{0:T(128)S(1)} %dynamic-update-slice.23), channel_id=1, replica_groups=mesh['img_0'=4,'img_1'=4,'tile_0'=4,'tile_1'=2] {'tile_1'}, use_global_device_ids=true, to_apply=%add.41 | all-reduce | flops 2 | bytes 16
  (356 shorter events, 261.1 us)
Async XLA Ops:
  2.3 38.5 %copy-start.21 = (f32[1,3,16,32,256]{4,3,2,1,0:T(8,128)S(1)}, f32[1,3,16,32,256]{4,3,2,1,0:T(8,128)}, u32[]{:S(2)}) copy-start(f32[1,3,16,32,256]{4,3,2,1,0:T(8,128)} %param.2) | copy-start | bytes 4718596
  2.3 37.2 %collective-permute-start = (f32[1,3,16,32,256]{4,2,3,1,0:T(8,128)S(1)}, f32[1,3,16,32,256]{4,2,3,1,0:T(8,128)S(1)}, u32[]{:S(2)}, u32[]{:S(2)}) collective-permute-start(f32[1,3,16,32,256]{4,2,3,1,0:T(8,128)S(1)} %copy.34), channel_id=1, source_target_pairs={{0,8},{8,16},{16,24},{24,32},{32,40},{40,48},{48,56},{56,64},{64,7... | collective-permute-start | bytes 4718600 | tf_op jit(solution)/shard_map/ppermute | solution.py:27
  6.6 36.8 %collective-permute-start.1 = (f32[1,3,16,32,256]{4,2,3,1,0:T(8,128)S(1)}, f32[1,3,16,32,256]{4,2,3,1,0:T(8,128)S(1)}, u32[]{:S(2)}, u32[]{:S(2)}) collective-permute-start(f32[1,3,16,32,256]{4,2,3,1,0:T(8,128)S(1)} %copy.34), channel_id=1, source_target_pairs={{8,0},{16,8},{24,16},{32,24},{40,32},{48,40},{56,48},{64,56},{72,6... | collective-permute-start | bytes 4718600 | tf_op jit(solution)/shard_map/ppermute | solution.py:29
  41.7 9.7 %copy-start.51 = (f32[16,32,256]{2,1,0:T(8,128)S(1)}, f32[16,32,256]{2,1,0:T(8,128)}, u32[]{:S(2)}) copy-start(f32[16,32,256]{2,1,0:T(8,128)} %param.3) | copy-start | bytes 1572868
  44.6 7.2 %copy-start.55 = (u32[128]{0:T(128)S(1)}, u32[128]{0:T(128)}, u32[]{:S(2)}) copy-start(u32[128]{0:T(128)} %constant.123) | copy-start | bytes 1540
  44.6 7.8 %collective-permute-start.2 = (f32[3,3,16,1,256]{4,2,3,1,0:T(8,128)S(1)}, f32[3,3,16,1,256]{4,2,3,1,0:T(8,128)S(1)}, u32[]{:S(2)}, u32[]{:S(2)}) collective-permute-start(f32[3,3,16,1,256]{4,2,3,1,0:T(8,128)S(1)} %get-tuple-element.73), channel_id=1, source_target_pairs={{0,1},{1,2},{2,3},{3,4},{4,5},{5,6},{6,7},{8,9},{9,10},{10,11},{11... | collective-permute-start | bytes 442376 | tf_op jit(solution)/shard_map/ppermute | solution.py:27
  49.5 6.5 collective-permute-start.3
  78.3 15.4 %all-to-all-start = ((f32[16,1,1]{2,1,0:T(1,128)}), f32[16,1,1]{2,1,0:T(1,128)S(1)}, u32[]{:S(2)}, u32[]{:S(2)}) async-start(f32[16,1,1]{2,1,0:T(1,128)} %broadcast_in_dim.22), calls=%async_computation | async-start | bytes 16384 | tf_op jit(solution)/shard_map/all_to_all | solution.py:38
  94.3 10.0 %all-to-all-start.1 = ((f32[16,1,1]{2,1,0:T(1,128)}), f32[16,1,1]{2,1,0:T(1,128)S(1)}, u32[]{:S(2)}, u32[]{:S(2)}) async-start(f32[16,1,1]{2,1,0:T(1,128)} %broadcast_in_dim.24), calls=%async_computation.1 | async-start | bytes 16384 | tf_op jit(solution)/shard_map/all_to_all | solution.py:38
  117.6 13.4 %collective-permute-start.4 = (f32[1,3,16,1,256]{4,2,3,1,0:T(8,128)S(1)}, f32[1,3,16,1,256]{4,2,3,1,0:T(8,128)S(1)}, u32[]{:S(2)}, u32[]{:S(2)}) collective-permute-start(f32[1,3,16,1,256]{4,2,3,1,0:T(8,128)S(1)} %get-tuple-element.103), channel_id=1, source_target_pairs={{0,1},{1,2},{2,3},{3,4},{4,5},{5,6},{6,7},{8,9},{9,10},{10,11},{11... | collective-permute-start | bytes 147464 | tf_op jit(solution)/shard_map/ppermute | solution.py:27
  123.6 7.5 %collective-permute-start.5 = (f32[1,3,16,1,256]{4,2,3,1,0:T(8,128)S(1)}, f32[1,3,16,1,256]{4,2,3,1,0:T(8,128)S(1)}, u32[]{:S(2)}, u32[]{:S(2)}) collective-permute-start(f32[1,3,16,1,256]{4,2,3,1,0:T(8,128)S(1)} %get-tuple-element.104), channel_id=1, source_target_pairs={{1,0},{2,1},{3,2},{4,3},{5,4},{6,5},{7,6},{9,8},{10,9},{11,10},{12... | collective-permute-start | bytes 147464 | tf_op jit(solution)/shard_map/ppermute | solution.py:29
  135.2 8.6 %copy-start.54 = (u32[128]{0:T(128)S(1)}, u32[128]{0:T(128)}, u32[]{:S(2)}) copy-start(u32[128]{0:T(128)} %constant.128) | copy-start | bytes 1540
  135.2 17.8 %copy-start.53 = (u32[128]{0:T(128)S(1)}, u32[128]{0:T(128)}, u32[]{:S(2)}) copy-start(u32[128]{0:T(128)} %constant.133) | copy-start | bytes 1540
  135.2 27.5 %copy-start.52 = (u32[128]{0:T(128)S(1)}, u32[128]{0:T(128)}, u32[]{:S(2)}) copy-start(u32[128]{0:T(128)} %constant.138) | copy-start | bytes 1540
  186.0 9.9 %copy-start.20 = (f32[1,3,16,32,256]{4,2,3,1,0:T(8,128)}, f32[1,3,16,32,256]{4,2,3,1,0:T(8,128)S(1)}, u32[]{:S(2)}) copy-start(f32[1,3,16,32,256]{4,2,3,1,0:T(8,128)S(1)} %divide_subtract_fusion.6) | copy-start | bytes 4718596
  186.1 4.3 collective-permute-start.6
  188.0 5.4 collective-permute-start.7
  206.4 7.2 %copy-start.47 = (f32[16,32,256]{2,0,1:T(8,128)S(1)}, f32[16,32,256]{2,0,1:T(8,128)}, u32[]{:S(2)}) copy-start(f32[16,32,256]{2,0,1:T(8,128)} %get-tuple-element.81) | copy-start | bytes 1572868
  208.8 5.0 collective-permute-start.8
  210.8 5.4 collective-permute-start.9
  261.7 10.0 %copy-start.17 = (f32[1,3,16,32,256]{4,2,3,1,0:T(8,128)}, f32[1,3,16,32,256]{4,2,3,1,0:T(8,128)S(1)}, u32[]{:S(2)}) copy-start(f32[1,3,16,32,256]{4,2,3,1,0:T(8,128)S(1)} %divide_subtract_fusion.5) | copy-start | bytes 4718596
  261.7 4.3 collective-permute-start.10
  263.7 5.4 collective-permute-start.11
  283.9 4.6 collective-permute-start.12
  286.0 5.4 collective-permute-start.13
  294.1 41.1 %copy-start.18 = (f32[1,3,16,32,256]{4,2,3,1,0:T(8,128)S(1)}, f32[1,3,16,32,256]{4,2,3,1,0:T(8,128)}, u32[]{:S(2)}) copy-start(f32[1,3,16,32,256]{4,2,3,1,0:T(8,128)} %copy-done.17) | copy-start | bytes 4718596
  337.0 49.2 %copy-start.9 = (f32[1,3,16,32,256]{4,2,3,1,0:T(8,128)}, f32[1,3,16,32,256]{4,2,3,1,0:T(8,128)S(1)}, u32[]{:S(2)}) copy-start(f32[1,3,16,32,256]{4,2,3,1,0:T(8,128)S(1)} %divide_subtract_fusion.4) | copy-start | bytes 4718596
  337.0 35.7 %collective-permute-start.14 = (f32[1,3,16,32,256]{4,2,3,1,0:T(8,128)S(1)}, f32[1,3,16,32,256]{4,2,3,1,0:T(8,128)S(1)}, u32[]{:S(2)}, u32[]{:S(2)}) collective-permute-start(f32[1,3,16,32,256]{4,2,3,1,0:T(8,128)S(1)} %divide_subtract_fusion.4), channel_id=1, source_target_pairs={{0,8},{8,16},{16,24},{24,32},{32,40},{40,48},{48,56},{56,64},{64,7... | collective-permute-start | bytes 4718600 | tf_op jit(solution)/shard_map/ppermute | solution.py:27
  339.4 37.2 %collective-permute-start.15 = (f32[1,3,16,32,256]{4,2,3,1,0:T(8,128)S(1)}, f32[1,3,16,32,256]{4,2,3,1,0:T(8,128)S(1)}, u32[]{:S(2)}, u32[]{:S(2)}) collective-permute-start(f32[1,3,16,32,256]{4,2,3,1,0:T(8,128)S(1)} %divide_subtract_fusion.4), channel_id=1, source_target_pairs={{8,0},{16,8},{24,16},{32,24},{40,32},{48,40},{56,48},{64,56},{72,6... | collective-permute-start | bytes 4718600 | tf_op jit(solution)/shard_map/ppermute | solution.py:29
  372.8 13.5 %copy-start.2 = (f32[1,3,16,32,256]{4,2,3,1,0:T(8,128)}, f32[1,3,16,32,256]{4,2,3,1,0:T(8,128)S(1)}, u32[]{:S(2)}) copy-start(f32[1,3,16,32,256]{4,2,3,1,0:T(8,128)S(1)} %collective-permute-done.14) | copy-start | bytes 4718596
  376.6 9.6 %copy-start.5 = (f32[1,3,16,32,256]{4,2,3,1,0:T(8,128)}, f32[1,3,16,32,256]{4,2,3,1,0:T(8,128)S(1)}, u32[]{:S(2)}) copy-start(f32[1,3,16,32,256]{4,2,3,1,0:T(8,128)S(1)} %collective-permute-done.15) | copy-start | bytes 4718596
  376.7 5.2 collective-permute-start.16
  379.8 6.5 collective-permute-start.17
  405.5 13.1 %all-to-all-start.2 = ((f32[16,1,1]{2,1,0:T(1,128)}), f32[16,1,1]{2,1,0:T(1,128)S(1)}, u32[]{:S(2)}, u32[]{:S(2)}) async-start(f32[16,1,1]{2,1,0:T(1,128)} %broadcast_in_dim.27), calls=%async_computation.2 | async-start | bytes 16384 | tf_op jit(solution)/shard_map/all_to_all | solution.py:38
  419.3 10.0 %all-to-all-start.3 = ((f32[16,1,1]{2,1,0:T(1,128)}), f32[16,1,1]{2,1,0:T(1,128)S(1)}, u32[]{:S(2)}, u32[]{:S(2)}) async-start(f32[16,1,1]{2,1,0:T(1,128)} %broadcast_in_dim.29), calls=%async_computation.3 | async-start | bytes 16384 | tf_op jit(solution)/shard_map/all_to_all | solution.py:38
  442.2 13.9 %collective-permute-start.18 = (f32[1,3,16,1,256]{4,2,3,1,0:T(8,128)S(1)}, f32[1,3,16,1,256]{4,2,3,1,0:T(8,128)S(1)}, u32[]{:S(2)}, u32[]{:S(2)}) collective-permute-start(f32[1,3,16,1,256]{4,2,3,1,0:T(8,128)S(1)} %get-tuple-element.91), channel_id=1, source_target_pairs={{0,1},{1,2},{2,3},{3,4},{4,5},{5,6},{6,7},{8,9},{9,10},{10,11},{11... | collective-permute-start | bytes 147464 | tf_op jit(solution)/shard_map/ppermute | solution.py:27
  448.5 7.5 %collective-permute-start.19 = (f32[1,3,16,1,256]{4,2,3,1,0:T(8,128)S(1)}, f32[1,3,16,1,256]{4,2,3,1,0:T(8,128)S(1)}, u32[]{:S(2)}, u32[]{:S(2)}) collective-permute-start(f32[1,3,16,1,256]{4,2,3,1,0:T(8,128)S(1)} %get-tuple-element.92), channel_id=1, source_target_pairs={{1,0},{2,1},{3,2},{4,3},{5,4},{6,5},{7,6},{9,8},{10,9},{11,10},{12... | collective-permute-start | bytes 147464 | tf_op jit(solution)/shard_map/ppermute | solution.py:29
  507.6 10.0 %copy-start.19 = (f32[1,3,16,32,256]{4,2,3,1,0:T(8,128)}, f32[1,3,16,32,256]{4,2,3,1,0:T(8,128)S(1)}, u32[]{:S(2)}) copy-start(f32[1,3,16,32,256]{4,2,3,1,0:T(8,128)S(1)} %divide_subtract_fusion.2) | copy-start | bytes 4718596
  507.7 4.3 collective-permute-start.20
  509.6 5.4 collective-permute-start.21
  530.4 4.6 collective-permute-start.22
  532.5 5.4 collective-permute-start.23
  583.2 10.0 %copy-start.15 = (f32[1,3,16,32,256]{4,2,3,1,0:T(8,128)}, f32[1,3,16,32,256]{4,2,3,1,0:T(8,128)S(1)}, u32[]{:S(2)}) copy-start(f32[1,3,16,32,256]{4,2,3,1,0:T(8,128)S(1)} %divide_subtract_fusion.1) | copy-start | bytes 4718596
  583.2 4.6 collective-permute-start.24
  585.1 5.4 collective-permute-start.25
  605.4 4.6 collective-permute-start.26
  607.4 5.4 collective-permute-start.27
  615.5 41.4 %copy-start.16 = (f32[1,3,16,32,256]{4,2,3,1,0:T(8,128)S(1)}, f32[1,3,16,32,256]{4,2,3,1,0:T(8,128)}, u32[]{:S(2)}) copy-start(f32[1,3,16,32,256]{4,2,3,1,0:T(8,128)} %copy-done.15) | copy-start | bytes 4718596
  (40 other events, 163.8 us)
